TPU v7x, 128 devices: a whole 4x4x4 slice. The times are simulated.
128 devices in a mesh: section: 8 (over z_lo, x), peer: 16 (over z_hi, y, core).
Axes of the slice: x: 4, y: 4, z: 4 (z_hi: 2, z_lo: 2; z = z_hi * 2 + z_lo), core: 2. Of those that a mesh axis runs over, the one named last changes fastest.
Arguments:
- acts: bfloat16 [8, 16, 384, 2560], P('section', 'peer'), may hold values from -6 to 6
- saved: bfloat16 [8, 16, 384, 2560], P('section', 'peer'), may hold values from -6 to 6
- cotangent: bfloat16 [8, 16, 384, 2560], P('section', 'peer'), may hold values from -6 to 6
- weight: bfloat16 [8, 2560, 2560], P('section', 'peer'), may hold values from -0.125 to 0.125
- gain: float32 [8, 2560], P('section'), may hold values from 0.1 to 1.9
- route: int32 [8, 16, 16, 1], P('section', 'peer'), may hold values from 0 to 15; in each aligned block of 16 rows (0 to 15, 16 to 31, ..., all dimensions but the last counted through in order) at most 2 rows name the same one
Outputs:
- next_acts: bfloat16 [8, 16, 768, 2560], P('section', 'peer')
- next_grads: bfloat16 [8, 16, 768, 2560], P('section', 'peer')
- weight_grad: float32 [8, 2560, 2560], P('section', 'peer')
Inputs may be any that keep to these rules, and one draw needn't show every extreme that they name: route[s, p, b, 0] is the peer that block b of peer p's forward arrival at section s is delivered to, and the peer of section s - 1 (the sections in a loop) that block b of its input gradient returns to. No peer is named more than 2 times among the 16 blocks of one peer, and in every draw some peer is named exactly 2 times.
All inputs are finite; a program needn't handle non-finite values.
Results may differ from a plain program's by a relative error of at most 0.015.
Values may be sent and summed in bfloat16 or wider, within the bound.
A program may use at most 128 MiB of HBM per device.

v0:
```python
import jax
import jax.numpy as jnp
from jax import lax
from jax.sharding import PartitionSpec as P

MOST = 2


EPS = 1e-05


def shifted(value, axis, steps):
    count = lax.axis_size(axis)
    pairs = [(source, (source + steps) % count) for source in range(count)]
    return lax.ppermute(value, axis, pairs)


def norm_rows(rows, gain_row):
    wide = rows.astype(jnp.float32)
    inverse = lax.rsqrt(jnp.mean(wide * wide, axis=-1, keepdims=True) + EPS)
    unit_rows = wide * inverse
    return ((unit_rows * gain_row).astype(jnp.bfloat16), unit_rows, inverse)


def silu_slope(values):
    sigma = jax.nn.sigmoid(values)
    return sigma * (1.0 + values * (1.0 - sigma))


def packing(route_row, peers, most):
    blocks_count = route_row.shape[0]
    row_order = lax.broadcasted_iota(jnp.int32, (blocks_count, blocks_count), 0)
    col_order = lax.broadcasted_iota(jnp.int32, (blocks_count, blocks_count), 1)
    matches = (route_row[:, None] == route_row[None, :]) & (col_order < row_order)
    ranking = jnp.sum(matches.astype(jnp.int32), axis=1)
    target = route_row * most + ranking
    slot_ids = lax.broadcasted_iota(jnp.int32, (peers * most, blocks_count), 0)
    return (slot_ids == target[None, :]).astype(jnp.bfloat16)


def pack_blocks(table, rows, most):
    blocks_count = table.shape[1]
    flat = rows.reshape(blocks_count, -1)
    packed = jnp.dot(table, flat, preferred_element_type=jnp.float32).astype(jnp.bfloat16)
    return packed.reshape(
        table.shape[0] // most, most * (rows.shape[0] // blocks_count), rows.shape[1]
    )


def local(acts, saved, cotangent, weight, gain, route):
    peers = lax.axis_size("peer")
    tokens_here = acts.shape[2]
    width = acts.shape[3]
    gain_row = gain[0]
    fresh = acts[0, 0]
    stored = saved[0, 0]
    upstream = cotangent[0, 0].astype(jnp.float32)
    normed_in = norm_rows(fresh, gain_row)[0]
    normed_saved, unit_saved, inv_saved = norm_rows(stored, gain_row)
    full_weight = lax.all_gather(weight[0], "peer", axis=0, tiled=True)
    pre_in = jnp.dot(normed_in, full_weight, preferred_element_type=jnp.float32)
    pre_saved = jnp.dot(normed_saved, full_weight, preferred_element_type=jnp.float32)
    output_rows = (fresh.astype(jnp.float32) + jax.nn.silu(pre_in)).astype(jnp.bfloat16)
    slope = (upstream * silu_slope(pre_saved)).astype(jnp.bfloat16)
    back_norm = lax.dot_general(
        slope, full_weight, (((1,), (1,)), ((), ())), preferred_element_type=jnp.float32
    )
    scaled = back_norm * gain_row
    centre = jnp.mean(scaled * unit_saved, axis=-1, keepdims=True)
    input_grad = (upstream + inv_saved * (scaled - unit_saved * centre)).astype(jnp.bfloat16)
    term = (
        lax.dot_general(
            normed_saved, slope, (((0,), (0,)), ((), ())), preferred_element_type=jnp.float32
        )
        / tokens_here
    )
    weight_grad = lax.psum_scatter(
        term.astype(jnp.bfloat16), "peer", scatter_dimension=0, tiled=True
    ).astype(jnp.float32)
    table = packing(route[0, 0, :, 0], peers, MOST)
    arrived = shifted(output_rows, "section", 1)
    landed = lax.all_to_all(
        pack_blocks(table, arrived, MOST), "peer", split_axis=0, concat_axis=0, tiled=True
    )
    returned = lax.all_to_all(
        pack_blocks(table, input_grad, MOST), "peer", split_axis=0, concat_axis=0, tiled=True
    )
    handed = shifted(returned, "section", -1)
    next_acts = landed.reshape(1, 1, -1, width)
    next_grads = handed.reshape(1, 1, -1, width)
    return (next_acts, next_grads, weight_grad[None])


def solution(mesh):
    placed = (
        P("section", "peer", None, None),
        P("section", "peer", None, None),
        P("section", "peer", None, None),
        P("section", "peer", None),
        P("section", None),
        P("section", "peer", None, None),
    )
    return jax.shard_map(
        local,
        mesh=mesh,
        in_specs=placed,
        out_specs=(
            P("section", "peer", None, None),
            P("section", "peer", None, None),
            P("section", "peer", None),
        ),
        check_vma=False,
    )
```

profile of v0, /device:TPU:6, one launch (start us, length us, event | category | flops | bytes accessed | tf_op | source)
XLA Modules:
  0.0 420.1 jit_solution(6469058449691822599)
XLA Ops:
  7.2 0.7 all-gather.3.cloned.1.call-update
  7.9 0.7 reduce
  8.7 2.0 fusion.18
  10.7 95.5 %all-gather.3.cloned.1.call-done = bf16[1,2560,2560]{2,1,0:T(8,128)(2,1)} async-done(((bf16[1,160,2560]{2,1,0:T(8,128)(2,1)}), bf16[1,2560,2560]{2,1,0:T(8,128)(2,1)}) %all-gather.3.cloned.1.call-update) | async-done | bytes 13107216 | tf_op jit(solution)/shard_map/all_gather | solution.py:60
  106.2 10.0 %fusion.12 = bf16[384,2560]{1,0:T(8,128)(2,1)S(1)} fusion(bf16[1,2560,2560]{2,1,0:T(8,128)(2,1)} %all-gather.3.cloned.1.call-done, bf16[1,1,384,2560]{3,2,1,0:T(8,128)(2,1)} %param.8, bf16[1,1,384,2560]{3,2,1,0:T(8,128)(2,1)} %param.7, f32[384]{0:T(512)S(1)} %add_rsqrt_fusion, f32[2560]{0:T(1024)S(1)} %reduce), kind=kOutput, calls=%fused_computation.20 | convolution fusion | flops 5046927360 | bytes 19017216 | tf_op jit(solution)/shard_map/dot_general | solution.py:62
  116.2 1.3 copy-done.4
  117.4 10.2 %multiply_convert_fusion = bf16[2560,2560]{1,0:T(8,128)(2,1)} fusion(bf16[384,2560]{1,0:T(8,128)(2,1)S(1)} %fusion.12, bf16[1,1,384,2560]{3,2,1,0:T(8,128)(2,1)S(1)} %copy-done, f32[384]{0:T(512)S(1)} %add_rsqrt_fusion, f32[2560]{0:T(1024)S(1)} %reduce), kind=kOutput, calls=%fused_computation.2 | convolution fusion | flops 5050204160 | bytes 17051136 | tf_op jit(solution)/shard_map/dot_general | solution.py:72
  128.5 2.0 fusion.19
  130.5 9.7 %fusion.15 = (f32[384]{0:T(512)S(1)}, f32[384,2560]{1,0:T(8,128)S(1)}) fusion(bf16[1,1,384,2560]{3,2,1,0:T(8,128)(2,1)S(1)} %copy-done, f32[384]{0:T(512)S(1)} %add_rsqrt_fusion, f32[2560]{0:T(1024)S(1)} %reduce, bf16[384,2560]{1,0:T(8,128)(2,1)} %copy-done.4, bf16[1,2560,2560]{2,1,0:T(8,128)(2,1)} %all-gather.3.cloned.1.call-done), kind=kOutput, calls=%fused_computation.23 | convolution fusion | flops 5038079488 | bytes 20984832 | tf_op jit(solution)/shard_map/dot_general | solution.py:65
  140.2 2.5 fusion.13
  142.7 2.3 reshape.63
  145.0 3.1 convolution_convert_fusion
  148.1 5.7 %reshape.64 = bf16[16,48,2560]{2,1,0:T(8,128)(2,1)} reshape(bf16[32,61440]{1,0:T(8,128)(2,1)} %convolution_convert_fusion) | data formatting | bytes 7864320 | tf_op jit(solution)/shard_map/reshape | solution.py:45
  153.8 4.9 %all-to-all-start.1 = ((bf16[16,48,2560]{2,1,0:T(8,128)(2,1)}), bf16[16,48,2560]{2,1,0:T(8,128)(2,1)}, u32[]{:S(2)}, u32[]{:S(2)}) async-start(bf16[16,48,2560]{2,1,0:T(8,128)(2,1)} %reshape.64), calls=%async_computation.1 | async-start | bytes 7864320 | tf_op jit(solution)/shard_map/all_to_all | solution.py:85
  158.7 8.8 %fusion.22 = bf16[384,2560]{1,0:T(8,128)(2,1)S(1)} fusion(bf16[1,2560,2560]{2,1,0:T(8,128)(2,1)} %all-gather.3.cloned.1.call-done, bf16[1,1,384,2560]{3,2,1,0:T(8,128)(2,1)S(1)} %copy-done.2, f32[2560]{0:T(1024)S(1)} %reduce, f32[384]{0:T(512)S(1)} %add_rsqrt_fusion.1), kind=kOutput, calls=%fused_computation.30 | convolution fusion | flops 5043978240 | bytes 17051136 | tf_op jit(solution)/shard_map/dot_general | solution.py:61
  167.9 66.7 %collective-permute-done = bf16[384,2560]{1,0:T(8,128)(2,1)} collective-permute-done((bf16[384,2560]{1,0:T(8,128)(2,1)S(1)}, bf16[384,2560]{1,0:T(8,128)(2,1)}, u32[]{:S(2)}, u32[]{:S(2)}) %collective-permute-start) | collective-permute-done | bytes 1966112 | tf_op jit(solution)/shard_map/ppermute | solution.py:15
  234.5 2.1 reshape.60
  236.8 3.1 convolution_convert_fusion.1
  239.8 5.4 %reshape.61 = bf16[16,48,2560]{2,1,0:T(8,128)(2,1)} reshape(bf16[32,61440]{1,0:T(8,128)(2,1)} %convolution_convert_fusion.1) | data formatting | bytes 7864320 | tf_op jit(solution)/shard_map/reshape | solution.py:45
  245.3 147.1 %all_to_all.10 = bf16[16,48,2560]{2,1,0:T(8,128)(2,1)} all-to-all(bf16[16,48,2560]{2,1,0:T(8,128)(2,1)} %reshape.61), channel_id=1, replica_groups=mesh['section'=8,'peer'=16] {'peer'}, dimensions={0} | all-to-all | bytes 7864320 | tf_op jit(solution)/shard_map/all_to_all | solution.py:82
  392.4 9.8 %reduce-scatter.2.cloned.1.call-done = bf16[160,2560]{1,0:T(8,128)(2,1)} async-done(((bf16[2560,2560]{1,0:T(8,128)(2,1)}), bf16[160,2560]{1,0:T(8,128)(2,1)}) %reduce-scatter.2.cloned.1.call-update) | async-done | bytes 819216 | tf_op jit(solution)/shard_map/reduce_scatter | solution.py:77
  402.2 2.5 bitcast_convert_fusion
  404.7 4.3 %copy.11 = bf16[1,1,768,2560]{3,2,1,0:T(8,128)(2,1)} copy(bf16[1,1,768,2560]{3,2,1,0:T(8,128)(2,1)} %bitcast.45) | data formatting | bytes 7864320
  409.0 4.3 %copy.12 = bf16[1,1,768,2560]{3,2,1,0:T(8,128)(2,1)} copy(bf16[1,1,768,2560]{3,2,1,0:T(8,128)(2,1)} %bitcast.9) | data formatting | bytes 7864320
  (21 shorter events, 1.4 us)
Async XLA Ops:
  7.2 99.0 %all-gather.3.cloned.1.call-start = ((), (), s32[]{:S(2)}) async-start(), calls=%async_computation.4 | async-start | bytes 13926400 | tf_op jit(solution)/shard_map/all_gather | solution.py:60
  7.9 394.3 %reduce-scatter.2.cloned.1.call-start = ((), (), s32[]{:S(2)}) async-start(), calls=%async_computation.3 | async-start | bytes 13926400 | tf_op jit(solution)/shard_map/reduce_scatter | solution.py:77
  10.7 106.7 %copy-start = (bf16[1,1,384,2560]{3,2,1,0:T(8,128)(2,1)S(1)}, bf16[1,1,384,2560]{3,2,1,0:T(8,128)(2,1)}, u32[]{:S(2)}) copy-start(bf16[1,1,384,2560]{3,2,1,0:T(8,128)(2,1)} %param.7) | copy-start | bytes 5898244
  116.2 1.3 copy-start.4
  127.6 0.7 copy-start.3
  130.5 9.7 %copy-start.1 = (bf16[1,1,384,2560]{3,2,1,0:T(8,128)(2,1)S(1)}, bf16[1,1,384,2560]{3,2,1,0:T(8,128)(2,1)}, u32[]{:S(2)}) copy-start(bf16[1,1,384,2560]{3,2,1,0:T(8,128)(2,1)} %param.8) | copy-start | bytes 5898244
  153.8 4.9 %copy-start.2 = (bf16[1,1,384,2560]{3,2,1,0:T(8,128)(2,1)S(1)}, bf16[1,1,384,2560]{3,2,1,0:T(8,128)(2,1)}, u32[]{:S(2)}) copy-start(bf16[1,1,384,2560]{3,2,1,0:T(8,128)(2,1)} %param.6) | copy-start | bytes 5898244
  153.8 82.9 %all-to-all-start.1 = ((bf16[16,48,2560]{2,1,0:T(8,128)(2,1)}), bf16[16,48,2560]{2,1,0:T(8,128)(2,1)}, u32[]{:S(2)}, u32[]{:S(2)}) async-start(bf16[16,48,2560]{2,1,0:T(8,128)(2,1)} %reshape.64), calls=%async_computation.1 | async-start | bytes 7864320 | tf_op jit(solution)/shard_map/all_to_all | solution.py:85
  167.5 67.0 %collective-permute-start = (bf16[384,2560]{1,0:T(8,128)(2,1)S(1)}, bf16[384,2560]{1,0:T(8,128)(2,1)}, u32[]{:S(2)}, u32[]{:S(2)}) collective-permute-start(bf16[384,2560]{1,0:T(8,128)(2,1)S(1)} %fusion.22), channel_id=1, source_target_pairs={{0,16},{16,32},{32,48},{48,64},{64,80},{80,96},{96,112},{112,0},{1... | collective-permute-start | bytes 5898248 | tf_op jit(solution)/shard_map/ppermute | solution.py:15
  236.7 155.7 %collective-permute-start.1 = (bf16[16,48,2560]{2,1,0:T(8,128)(2,1)}, bf16[16,48,2560]{2,1,0:T(8,128)(2,1)}, u32[]{:S(2)}, u32[]{:S(2)}) collective-permute-start(bf16[16,48,2560]{2,1,0:T(8,128)(2,1)} %all-to-all-done.1), channel_id=1, source_target_pairs={{0,112},{16,0},{32,16},{48,32},{64,48},{80,64},{96,80},{112,96},{1... | collective-permute-start | bytes 11796488 | tf_op jit(solution)/shard_map/ppermute | solution.py:15
Sparse Core Ops, SparseCore 0:
  10.4 95.7 all-gather.2
  127.8 274.3 reduce-scatter.1
where the time goes:
time: 421 us; the launch traced here: 420 us
  waiting for transfers between devices  173 us (41%)
  blocking collectives  147 us (35%)
  matrix products  44.8 us (11%)
  local copies, waits for them, and re-layouts  26 us (6%)
  between operations  14.2 us (3%)
  other arithmetic  9.97 us (2%)
  starting transfers between devices  5.34 us (1%)
    all_to_all x1, blocking collectives, local(): lax.all_to_all(pack_blocks(table, arrived, MOST), 'peer', split_axis=0, c...  147 us
    all_gather x1, waiting for transfers between devices, local(): full_weight = lax.all_gather(weight[0], 'peer', axis=0, tiled=True)  95.5 us
    ppermute x2, waiting for transfers between devices, shifted(): return lax.ppermute(value, axis, pairs)  66.7 us
    reshape x2, local copies, waits for them, and re-layouts, pack_blocks(): packed.reshape(table.shape[0] // most, most * (rows.shape[0] // blocks_co...  11.1 us
    unnamed x12, local copies, waits for them, and re-layouts  10.5 us
    dot_general x1, matrix products, local(): lax.dot_general(normed_saved, slope, (((0,), (0,)), ((), ())), preferred_...  10.2 us
    dot_general x1, matrix products, local(): jnp.dot(normed_saved, full_weight, preferred_element_type=jnp.float32)  9.97 us
    reduce_scatter x1, waiting for transfers between devices, local(): lax.psum_scatter(term.astype(jnp.bfloat16), 'peer', scatter_dimension=0,...  9.81 us
  transfers between devices with their start and end apart: 5, of which 3 were waited for; matrix products, arithmetic and copies ran while one was open for 11% of the time, Pallas kernels for 0%

commit v1 on v0

v1 whole, which is shorter than its diff:
```python
import functools

import jax
import jax.numpy as jnp
from jax import lax
from jax.experimental import pallas as pl
from jax.experimental.pallas import tpu as pltpu
from jax.sharding import PartitionSpec as P

MESH = pl.DeviceIdType.MESH
F32 = jnp.float32
BF16 = jnp.bfloat16
MOST = 2
EPS = 1e-05

A = 96

ORDER = (
    (1, 2, 0), (1, 2, 1), (0, 2, 0), (1, 1, 0), (0, 3, 1), (1, 3, 0), (0, 1, 1), (1, 1, 1),
    (0, 3, 0), (1, 3, 1), (0, 1, 0), (0, 2, 1), (1, 0, 0), (1, 0, 1), (0, 0, 1),
)
SLOTS = 96


def kernel(
    acts, saved, cot, w, gain, route,
    next_acts, next_grads, wgrad,
    full, acts_v, saved_v, cot_v, chunks, acc, turned, turned_out, slopes, inverse,
    terms, half_a, side_a, far_a, far_b, half_b, side_b, rows_f, rows_b, perm, targets, targets_next,
    send_sem, recv_sem, local_sem,
):
    shard, width = w.shape
    tokens = acts.shape[0]
    chip = 2 * shard
    sections = lax.axis_size("section")
    s = lax.axis_index("section")
    p = lax.axis_index("peer")
    zh, y, c = p // 8, lax.rem(p // 2, 4), lax.rem(p, 2)
    zo, co = 1 - zh, 1 - c
    yp, ym, y2 = lax.rem(y + 1, 4), lax.rem(y + 3, 4), lax.rem(y + 2, 4)
    sp, sm = lax.rem(s + 1, sections), lax.rem(s + sections - 1, sections)

    def peer(zz, yy, cc):
        return (s, zz * 8 + yy * 2 + cc)

    right, left, across, core = peer(zh, yp, c), peer(zh, ym, c), peer(zo, y, c), peer(zh, y, co)

    tags = {}
    sent = []

    def slot(tag):
        return tags.setdefault(tag, len(tags))

    def send(tag, src, dst, device):
        copy = pltpu.make_async_remote_copy(
            src_ref=src, dst_ref=dst, send_sem=send_sem.at[slot(tag)],
            recv_sem=recv_sem.at[slot(tag)], device_id=device, device_id_type=MESH,
        )
        copy.start()
        sent.append(copy)
        return copy

    def arrive(tag, dst):
        pltpu.make_async_remote_copy(
            src_ref=dst, dst_ref=dst, send_sem=send_sem.at[slot(tag)],
            recv_sem=recv_sem.at[slot(tag)], device_id=core, device_id_type=MESH,
        ).wait_recv()

    loads = [
        pltpu.make_async_copy(src, dst, local_sem.at[i])
        for i, (src, dst) in enumerate(((saved, saved_v), (acts, acts_v), (cot, cot_v)))
    ]
    base = pl.multiple_of(p * shard, 32)
    own_rows = pltpu.make_async_copy(w, full.at[pl.ds(base, shard)], local_sem.at[3])
    own_rows.start()
    for copy in loads:
        copy.start()

    barrier = pltpu.get_barrier_semaphore()
    friends = [peer(zh ^ dz, lax.rem(y + dy, 4), c ^ dc) for dz, dy, dc in ORDER] + [(sp, p), (sm, p)]
    for device in friends:
        pl.semaphore_signal(barrier, inc=1, device_id=device, device_id_type=MESH)
    pl.semaphore_wait(barrier, len(friends))

    def region(zz, yy, cc, lo, hi):
        start = pl.multiple_of((zz * 8 + yy * 2 + cc) * shard + lo, 16)
        return full.at[pl.ds(start, hi - lo)]

    H, M = A // 2, A + (shard - A) // 2
    pieces = {
        "own": (zh, y, 0, shard),
        "zA": (zo, y, 0, A), "yA+": (zh, ym, 0, A), "yA-": (zh, yp, 0, A),
        "yB+": (zh, ym, A, shard), "yB-": (zh, yp, A, shard), "zB": (zo, y, A, shard),
        "A0": (zh, y2, 0, H), "A1": (zh, y2, H, A), "B0": (zh, y2, A, M), "B1": (zh, y2, M, shard),
        "wA+": (zo, ym, 0, A), "wA-": (zo, yp, 0, A), "wA0": (zo, y2, 0, H), "wA1": (zo, y2, H, A),
        "zB+": (zo, ym, A, shard), "zB-": (zo, yp, A, shard),
        "zB0": (zo, y2, A, M), "zB1": (zo, y2, M, shard),
    }

    def give(tag, lo, hi, device):
        send(tag, w.at[pl.ds(lo, hi - lo)], region(zh, y, c, lo, hi), device)

    give("yA+", 0, A, right)
    give("zA", 0, A, across)
    give("yA-", 0, A, left)
    give("yB+", A, shard, right)
    give("zB", A, shard, across)
    give("yB-", A, shard, left)
    give("c:own", 0, shard, core)

    def pass_on(tag, *onward):
        zz, yy, lo, hi = pieces[tag]
        arrive(tag, region(zz, yy, c, lo, hi))
        for new, device in onward:
            _, _, nlo, nhi = pieces[new] if new in ("A0", "A1", "B0", "B1", "wA0", "wA1") else pieces[tag]
            part = region(zz, yy, c, nlo, nhi)
            send(new, part, part, device)
        part = region(zz, yy, c, lo, hi)
        send("c:" + tag, part, part, core)

    def from_core(*names):
        for tag in names:
            zz, yy, lo, hi = pieces[tag]
            arrive("c:" + tag, region(zz, yy, co, lo, hi))

    named = [route[b] for b in range(route.shape[0])]
    block = tokens // len(named)
    lane = lax.broadcasted_iota(jnp.int32, targets.shape, 1)
    spot = jnp.zeros(targets.shape, jnp.int32)
    for b, r in enumerate(named):
        rank = jnp.int32(0)
        for other in named[:b]:
            rank = rank + jnp.where(other == r, 1, 0).astype(jnp.int32)
        first = (r * MOST + rank) * block - b * block
        spot = jnp.where((lane >= b * block) & (lane < (b + 1) * block), lane + first, spot)
    targets[...] = spot
    send("targets", targets, targets_next, (sm, p))

    gain_row = gain[...]
    step_rows = 32

    def normalise(source, offset, keep):
        def body(i, carry):
            at = pl.ds(pl.multiple_of(i * step_rows, step_rows), step_rows)
            wide = source[at, :].astype(F32)
            inv = lax.rsqrt(jnp.mean(wide * wide, axis=-1, keepdims=True) + EPS)
            normed = (wide * inv * gain_row).astype(BF16)
            to = pl.ds(pl.multiple_of(offset + i * step_rows, step_rows), step_rows)
            for k in range(width // chip):
                chunks[k, to, :] = normed[:, k * chip:(k + 1) * chip]
            if keep:
                inverse[at, :] = jnp.broadcast_to(inv, (step_rows, inverse.shape[1]))
            return carry

        lax.fori_loop(0, tokens // step_rows, body, 0)

    loads[0].wait()
    normalise(saved_v, 0, True)
    loads[1].wait()
    normalise(acts_v, tokens, False)

    columns = 512

    def multiply(zz, yy, start=False):
        k = zz * 4 + yy
        at = pl.ds(pl.multiple_of(k * chip, 64), chip)

        def body(i, carry):
            cols = pl.ds(pl.multiple_of(i * columns, columns), columns)
            part = jnp.dot(chunks[k], full[at, cols], preferred_element_type=F32)
            acc[:, cols] = part if start else acc[:, cols] + part
            return carry

        lax.fori_loop(0, width // columns, body, 0)

    own_rows.wait()
    from_core("own")
    multiply(zh, y, True)

    pass_on("zA", ("wA+", right), ("wA-", left))
    pass_on("yA+", ("A0", right))
    pass_on("yA-", ("A1", left))

    def turn(k, carry):
        flat = jnp.transpose(chunks[k, 0:tokens, :].astype(F32)).astype(BF16)
        low, high = flat[:shard], flat[shard:]
        to = pl.ds(pl.multiple_of((lax.rem(k, 4) * 2 + k // 4) * shard, 32), shard)
        turned[to, 0:tokens] = jnp.where(c == 0, low, high)
        turned_out[to, :] = jnp.where(c == 0, high, low)
        return carry

    lax.fori_loop(0, width // chip, turn, 0)
    send("turned", turned_out, turned.at[:, pl.ds(tokens, tokens)], core)

    pass_on("yB+", ("B0", right), ("zB+", across))
    pass_on("yB-", ("B1", left), ("zB-", across))
    pass_on("zB")
    from_core("yA+", "yB+")
    multiply(zh, ym)
    pass_on("A0")
    pass_on("A1")
    from_core("yA-", "yB-")
    multiply(zh, yp)
    pass_on("B0", ("zB0", across))
    pass_on("B1", ("zB1", across))
    from_core("zA", "zB")
    multiply(zo, y)
    pass_on("wA+", ("wA0", right))
    pass_on("wA-", ("wA1", left))
    from_core("A0", "A1", "B0", "B1")
    multiply(zh, y2)
    pass_on("zB+")
    pass_on("zB-")
    from_core("wA+", "zB+")
    multiply(zo, ym)
    pass_on("zB0")
    pass_on("zB1")
    from_core("wA-", "zB-")
    multiply(zo, yp)
    pass_on("wA0")
    pass_on("wA1")
    from_core("wA0", "wA1", "zB0", "zB1")
    multiply(zo, y2)

    loads[2].wait()
    gathered = list(sent)
    sent.clear()

    def slope_body(i, carry):
        at = pl.ds(pl.multiple_of(i * step_rows, step_rows), step_rows)
        v = acc[at, :]
        sigma = jax.nn.sigmoid(v)
        slopes[at, :] = (cot_v[at, :].astype(F32) * (sigma * (1.0 + v * (1.0 - sigma)))).astype(BF16)
        return carry

    lax.fori_loop(0, tokens // step_rows, slope_body, 0)
    send("slope", slopes.at[pl.ds(0, tokens)], slopes.at[pl.ds(tokens, tokens)], core)

    def output_body(i, carry):
        at = pl.ds(pl.multiple_of(i * step_rows, step_rows), step_rows)
        v = acc[pl.ds(pl.multiple_of(tokens + i * step_rows, step_rows), step_rows), :]
        acts_v[at, :] = (acts_v[at, :].astype(F32) + v * jax.nn.sigmoid(v)).astype(BF16)
        return carry

    lax.fori_loop(0, tokens // step_rows, output_body, 0)
    send("forward", acts_v, rows_f, (sp, p))

    arrive("turned", turned.at[:, pl.ds(tokens, tokens)])
    arrive("slope", slopes.at[pl.ds(tokens, tokens)])

    def term(k, yy):
        at = pl.ds(pl.multiple_of(yy * chip, 64), chip)

        def body(i, carry):
            cols = pl.ds(pl.multiple_of(i * columns, columns), columns)
            part = jnp.dot(turned[at, :], slopes[:, cols], preferred_element_type=F32) / tokens
            part = part.astype(BF16)
            terms[k, 0, :, cols] = part[:shard]
            terms[k, 1, :, cols] = part[shard:]
            return carry

        lax.fori_loop(0, width // columns, body, 0)

    def cross(k):
        send("tB%d" % k, terms.at[k, zo, pl.ds(A, shard - A)], far_b.at[k], across)

    lower, upper = pl.ds(0, H), pl.ds(H, H)
    last, last_low, last_high = pl.ds(A, shard - A), pl.ds(A, M - A), pl.ds(M, shard - M)
    term(0, y2)
    send("tA0", terms.at[0, :, lower], half_a.at[0], right)
    send("tA1", terms.at[0, :, upper], half_a.at[1], left)
    cross(0)
    term(1, yp)
    cross(1)
    term(2, ym)
    cross(2)
    term(3, y)
    cross(3)

    tile = 256

    def back_body(i, carry):
        at = pl.ds(pl.multiple_of(i * tile, tile), tile)
        acc[0:tokens, at] = lax.dot_general(
            slopes[0:tokens, :], full[at, :], (((1,), (1,)), ((), ())), preferred_element_type=F32
        )
        return carry

    lax.fori_loop(0, width // tile, back_body, 0)

    def add(target, lo, count, extra):
        size = 16

        def body(i, carry):
            at = pl.ds(pl.multiple_of(lo + i * size, size), size)
            here = pl.ds(pl.multiple_of(i * size, size), size)
            target[at, :] = (target[at, :].astype(F32) + extra[here, :].astype(F32)).astype(BF16)
            return carry

        lax.fori_loop(0, count // size, body, 0)

    arrive("tB0", far_b.at[0])
    add(terms.at[0, zh], A, shard - A, far_b.at[0])
    send("tb0", terms.at[0, zh, last_low], half_b.at[0], right)
    send("tb1", terms.at[0, zh, last_high], half_b.at[1], left)
    arrive("tA0", half_a.at[0])
    for z in range(2):
        add(terms.at[1, z], 0, H, half_a.at[0, z])
    send("tA+", terms.at[1, :, pl.ds(0, A)], side_a.at[0], right)
    arrive("tA1", half_a.at[1])
    for z in range(2):
        add(terms.at[2, z], H, H, half_a.at[1, z])
    send("tA-", terms.at[2, :, pl.ds(0, A)], side_a.at[1], left)

    def grad_body(i, carry):
        at = pl.ds(pl.multiple_of(i * step_rows, step_rows), step_rows)
        scaled = acc[at, :] * gain_row
        inv = inverse[at, 0:1]
        unit = saved_v[at, :].astype(F32) * inv
        centre = jnp.mean(scaled * unit, axis=-1, keepdims=True)
        cot_v[at, :] = (cot_v[at, :].astype(F32) + inv * (scaled - unit * centre)).astype(BF16)
        return carry

    lax.fori_loop(0, tokens // step_rows, grad_body, 0)
    send("backward", cot_v, rows_b, (sm, p))

    for k, tag, lo, count, device in ((1, "tb0", A, M - A, right), (2, "tb1", M, shard - M, left)):
        arrive("tB%d" % k, far_b.at[k])
        add(terms.at[k, zh], A, shard - A, far_b.at[k])
        arrive(tag, half_b.at[k - 1])
        add(terms.at[k, zh], lo, count, half_b.at[k - 1])
        send("tB" + "?+-"[k], terms.at[k, zh, last], side_b.at[k - 1], device)

    def pack(rows, where, at_row):
        size = 96

        def build(i, carry):
            at = pl.ds(pl.multiple_of(i * size, size), size)
            row = lax.broadcasted_iota(jnp.int32, (size, tokens), 0) + i * size
            perm[at, :] = jnp.where(row == where[0:1, :], 1.0, 0.0).astype(BF16)
            return carry

        lax.fori_loop(0, perm.shape[0] // size, build, 0)

        def body(i, carry):
            cols = pl.ds(pl.multiple_of(i * columns, columns), columns)
            full[at_row:at_row + perm.shape[0], cols] = jnp.dot(
                perm[...], rows[:, cols], preferred_element_type=F32
            ).astype(BF16)
            return carry

        lax.fori_loop(0, width // columns, body, 0)

    share = MOST * block

    def place(ref, number, offset=0):
        return ref.at[pl.ds(pl.multiple_of(offset + number * share, 16), share)]

    def scatter(name, out, offset, sem):
        local = pltpu.make_async_copy(place(full, p, offset), place(out, p), local_sem.at[sem])
        for i, (dz, dy, dc) in enumerate(ORDER):
            to = peer(zh ^ dz, lax.rem(y + dy, 4), c ^ dc)
            send("%s%d" % (name, i), place(full, to[1], offset), place(out, p), to)
        local.start()
        return local

    def collect(name, out):
        for i, (dz, dy, dc) in enumerate(ORDER):
            origin = peer(zh ^ dz, lax.rem(y + 4 - dy, 4), c ^ dc)
            arrive("%s%d" % (name, i), place(out, origin[1]))

    for copy in gathered:
        copy.wait_send()

    arrive("tA+", side_a.at[0])
    arrive("tA-", side_a.at[1])
    for z in range(2):
        add(terms.at[3, z], 0, A, side_a.at[0, z])
        add(terms.at[3, z], 0, A, side_a.at[1, z])
    send("tzA", terms.at[3, zo, pl.ds(0, A)], far_a, across)

    arrive("forward", rows_f)
    pack(rows_f, targets, 0)
    local_f = scatter("f", next_acts, 0, 4)
    arrive("targets", targets_next)
    arrive("backward", rows_b)
    pack(rows_b, targets_next, perm.shape[0])
    local_b = scatter("b", next_grads, perm.shape[0], 5)

    arrive("tzA", far_a)
    arrive("tB3", far_b.at[3])
    arrive("tB+", side_b.at[0])
    arrive("tB-", side_b.at[1])
    size = 16

    def last_a(i, carry):
        at = pl.ds(pl.multiple_of(i * size, size), size)
        to = pl.ds(pl.multiple_of(tokens + i * size, size), size)
        acc[to, :] = terms[3, zh, at, :].astype(F32) + far_a[at, :].astype(F32)
        return carry

    lax.fori_loop(0, A // size, last_a, 0)

    def last_b(i, carry):
        here = pl.ds(pl.multiple_of(i * size, size), size)
        at = pl.ds(pl.multiple_of(A + i * size, size), size)
        to = pl.ds(pl.multiple_of(tokens + A + i * size, size), size)
        acc[to, :] = (
            (terms[3, zh, at, :].astype(F32) + far_b[3, here, :].astype(F32))
            + (side_b[0, here, :].astype(F32) + side_b[1, here, :].astype(F32))
        )
        return carry

    lax.fori_loop(0, (shard - A) // size, last_b, 0)
    store = pltpu.make_async_copy(acc.at[pl.ds(tokens, shard)], wgrad, local_sem.at[6])
    store.start()

    collect("f", next_acts)
    collect("b", next_grads)
    store.wait()
    local_f.wait()
    local_b.wait()
    for copy in sent:
        copy.wait_send()
    assert len(tags) <= SLOTS, len(tags)


def local(acts, saved, cotangent, weight, gain, route):
    tokens, width = acts.shape[2:]
    shard = weight.shape[1]
    peers = width // shard
    packed = MOST * tokens
    hbm = pl.BlockSpec(memory_space=pl.ANY)
    v = pltpu.VMEM
    next_acts, next_grads, weight_grad = pl.pallas_call(
        kernel,
        out_shape=(
            jax.ShapeDtypeStruct((packed, width), BF16),
            jax.ShapeDtypeStruct((packed, width), BF16),
            jax.ShapeDtypeStruct((shard, width), F32),
        ),
        in_specs=[hbm] * 4 + [pl.BlockSpec(memory_space=v), pl.BlockSpec(memory_space=pltpu.SMEM)],
        out_specs=(hbm, hbm, hbm),
        scratch_shapes=[
            v((width, width), BF16),
            v((tokens, width), BF16), v((tokens, width), BF16), v((tokens, width), BF16),
            v((peers // 2, 2 * tokens, 2 * shard), BF16),
            v((2 * tokens, width), F32),
            v((width // 2, 2 * tokens), BF16), v((width // 2, tokens), BF16),
            v((2 * tokens, width), BF16),
            v((tokens, 128), F32),
            v((4, 2, shard, width), BF16),
            v((2, 2, A // 2, width), BF16),
            v((2, 2, A, width), BF16),
            v((A, width), BF16),
            v((4, shard - A, width), BF16),
            v((2, (shard - A) // 2, width), BF16),
            v((2, shard - A, width), BF16),
            v((tokens, width), BF16), v((tokens, width), BF16),
            v((packed, tokens), BF16),
            v((8, tokens), jnp.int32), v((8, tokens), jnp.int32),
            pltpu.SemaphoreType.DMA((SLOTS,)),
            pltpu.SemaphoreType.DMA((SLOTS,)),
            pltpu.SemaphoreType.DMA((8,)),
        ],
        compiler_params=pltpu.CompilerParams(
            collective_id=0, has_side_effects=True, vmem_limit_bytes=62 << 20
        ),
        name="tick",
    )(acts[0, 0], saved[0, 0], cotangent[0, 0], weight[0], gain, route[0, 0, :, 0])
    return (next_acts[None, None], next_grads[None, None], weight_grad[None])


def solution(mesh):
    placed = (
        P("section", "peer", None, None),
        P("section", "peer", None, None),
        P("section", "peer", None, None),
        P("section", "peer", None),
        P("section", None),
        P("section", "peer", None, None),
    )
    return jax.shard_map(
        local,
        mesh=mesh,
        in_specs=placed,
        out_specs=(
            P("section", "peer", None, None),
            P("section", "peer", None, None),
            P("section", "peer", None),
        ),
        check_vma=False,
    )
```

time: 421 us -> 262 us (0.62)
  Pallas kernels: 0 us -> 252 us
  waiting for transfers between devices: 173 us -> 0 us
  blocking collectives: 147 us -> 0 us
  matrix products: 44.8 us -> 0 us
  local copies, waits for them, and re-layouts: 26 us -> 8.22 us
  between operations: 14.2 us -> 0.65 us
  other arithmetic: 9.97 us -> 0 us
  starting transfers between devices: 5.34 us -> 0 us
    pallas_call x0 -> x1, Pallas kernels: none -> 252 us  [local(): pl.pallas_call(kernel, out_shape=(jax.ShapeDtypeStruct((packed, width), B...]
    all_to_all x1 -> x0, blocking collectives: 147 us -> none  [local(): lax.all_to_all(pack_blocks(table, arrived, MOST), 'peer', split_axis=0, c...]
    all_gather x1 -> x0, waiting for transfers between devices: 95.5 us -> none  [local(): full_weight = lax.all_gather(weight[0], 'peer', axis=0, tiled=True)]
    ppermute x2 -> x0, waiting for transfers between devices: 66.7 us -> none  [shifted(): return lax.ppermute(value, axis, pairs)]
    dot_general x6 -> x0, matrix products: 44.8 us -> none  [the longest x1 10.2 us: local(): lax.dot_general(normed_saved, slope, (((0,), (0,)), ((), ())), preferred_...]
    reshape x4 -> x0, local copies, waits for them, and re-layouts: 15.5 us -> none  [the longest x2 11.1 us: pack_blocks(): packed.reshape(table.shape[0] // most, most * (rows.shape[0] // blocks_co...]
    reduce_scatter x1 -> x0, waiting for transfers between devices: 9.81 us -> none  [local(): lax.psum_scatter(term.astype(jnp.bfloat16), 'peer', scatter_dimension=0,...]
    all_to_all x1 -> x0, starting transfers between devices: 4.85 us -> none  [local(): lax.all_to_all(pack_blocks(table, input_grad, MOST), 'peer', split_axis=0...]
  transfers between devices with their start and end apart: 5 -> 0, of which waited for: 3 -> 0; matrix products, arithmetic and copies ran while one was open for 11% -> 0% of each run, Pallas kernels for 0% -> 0%
where the time goes in v1:
time: 262 us; the launch traced here: 261 us
  Pallas kernels  252 us (96%)
  local copies, waits for them, and re-layouts  8.22 us (3%)
    pallas_call x1, Pallas kernels, local(): pl.pallas_call(kernel, out_shape=(jax.ShapeDtypeStruct((packed, width), B...  252 us
    unnamed x7, local copies, waits for them, and re-layouts  8.22 us

profile of v1, /device:TPU:6, one launch (start us, length us, event | category | flops | bytes accessed | tf_op | source)
XLA Modules:
  0.0 261.0 jit_solution(5457122779547919925)
XLA Ops:
  0.6 252.1 %tick.1 = (bf16[768,2560]{1,0:T(8,128)(2,1)}, bf16[768,2560]{1,0:T(8,128)(2,1)}, f32[160,2560]{1,0:T(8,128)}) custom-call(bf16[384,2560]{1,0:T(8,128)(2,1)} %bitcast.10, bf16[384,2560]{1,0:T(8,128)(2,1)} %bitcast.11, bf16[384,2560]{1,0:T(8,128)(2,1)} %bitcast.12, bf16[160,2560]{1,0:T(8,128)(2,1)} %bitcast.14, f32[1,2560]{1,0:T(1,128)} %gain.1, s32[16]{0:T(128)} %bitcast.15), custom_call_target="tpu_custom_call" | custom-call | tf_op jit(solution)/shard_map/tick/pallas_call | solution.py:435
  252.7 0.0 copy-start
  252.8 4.4 %copy.12 = bf16[1,1,768,2560]{3,2,1,0:T(8,128)(2,1)} copy(bf16[1,1,768,2560]{3,2,1,0:T(8,128)(2,1)} %bitcast.9) | data formatting | bytes 7864320
  257.2 0.0 copy-done
  257.2 0.0 copy-start.1
  257.2 1.9 copy.13
  259.1 0.7 copy-done.1
  259.8 1.2 copy.14
Async XLA Ops:
  252.7 4.5 %copy-start = (bf16[768,2560]{1,0:T(8,128)(2,1)S(1)}, bf16[768,2560]{1,0:T(8,128)(2,1)}, u32[]{:S(2)}) copy-start(bf16[768,2560]{1,0:T(8,128)(2,1)} %get-tuple-element.7) | copy-start | bytes 11796484
  257.2 2.6 %copy-start.1 = (f32[160,2560]{1,0:T(8,128)S(1)}, f32[160,2560]{1,0:T(8,128)}, u32[]{:S(2)}) copy-start(f32[160,2560]{1,0:T(8,128)} %get-tuple-element.8) | copy-start | bytes 4915204

commit v2 on v1

--- a/solution.py
+++ b/solution.py
@@ -26,19 +26,19 @@
     acts, saved, cot, w, gain, route,
     next_acts, next_grads, wgrad,
     full, acts_v, saved_v, cot_v, chunks, acc, turned, turned_out, slopes, inverse,
-    terms, half_a, side_a, far_a, far_b, half_b, side_b, rows_f, rows_b, perm, targets, targets_next,
+    terms, half_a, side_a, far_a, far_b, half_b, side_b, rows_f, rows_b, perm, targets, targets_next, targets_flip,
     send_sem, recv_sem, local_sem,
 ):
     shard, width = w.shape
     tokens = acts.shape[0]
     chip = 2 * shard
-    sections = lax.axis_size("section")
     s = lax.axis_index("section")
     p = lax.axis_index("peer")
     zh, y, c = p // 8, lax.rem(p // 2, 4), lax.rem(p, 2)
     zo, co = 1 - zh, 1 - c
     yp, ym, y2 = lax.rem(y + 1, 4), lax.rem(y + 3, 4), lax.rem(y + 2, 4)
-    sp, sm = lax.rem(s + 1, sections), lax.rem(s + sections - 1, sections)
+    x, low = lax.rem(s, 4), (s // 4) * 4
+    xp, xm, flipped = low + lax.rem(x + 1, 4), low + lax.rem(x + 3, 4), 4 - low + x
 
     def peer(zz, yy, cc):
         return (s, zz * 8 + yy * 2 + cc)
@@ -46,7 +46,7 @@
     right, left, across, core = peer(zh, yp, c), peer(zh, ym, c), peer(zo, y, c), peer(zh, y, co)
 
     tags = {}
-    sent = []
+    sent = {}
 
     def slot(tag):
         return tags.setdefault(tag, len(tags))
@@ -57,8 +57,12 @@
             recv_sem=recv_sem.at[slot(tag)], device_id=device, device_id_type=MESH,
         )
         copy.start()
-        sent.append(copy)
-        return copy
+        sent[tag] = copy
+
+    def finished(*names):
+        for tag in names:
+            copy = sent.pop(tag)
+            copy.wait_send()
 
     def arrive(tag, dst):
         pltpu.make_async_remote_copy(
@@ -77,7 +81,8 @@
         copy.start()
 
     barrier = pltpu.get_barrier_semaphore()
-    friends = [peer(zh ^ dz, lax.rem(y + dy, 4), c ^ dc) for dz, dy, dc in ORDER] + [(sp, p), (sm, p)]
+    friends = [peer(zh ^ dz, lax.rem(y + dy, 4), c ^ dc) for dz, dy, dc in ORDER] + [(xp, p), (xm, p)]
+    friends += [(flipped, i) for i in range(16)]
     for device in friends:
         pl.semaphore_signal(barrier, inc=1, device_id=device, device_id_type=MESH)
     pl.semaphore_wait(barrier, len(friends))
@@ -134,7 +139,8 @@
         first = (r * MOST + rank) * block - b * block
         spot = jnp.where((lane >= b * block) & (lane < (b + 1) * block), lane + first, spot)
     targets[...] = spot
-    send("targets", targets, targets_next, (sm, p))
+    send("targets", targets, targets_next, (xm, p))
+    send("flip", targets, targets_flip, (flipped, p))
 
     gain_row = gain[...]
     step_rows = 32
@@ -224,7 +230,6 @@
 
     loads[2].wait()
     gathered = list(sent)
-    sent.clear()
 
     def slope_body(i, carry):
         at = pl.ds(pl.multiple_of(i * step_rows, step_rows), step_rows)
@@ -243,7 +248,7 @@
         return carry
 
     lax.fori_loop(0, tokens // step_rows, output_body, 0)
-    send("forward", acts_v, rows_f, (sp, p))
+    send("forward", acts_v, rows_f, (xp, p))
 
     arrive("turned", turned.at[:, pl.ds(tokens, tokens)])
     arrive("slope", slopes.at[pl.ds(tokens, tokens)])
@@ -288,6 +293,18 @@
 
     lax.fori_loop(0, width // tile, back_body, 0)
 
+    def grad_body(i, carry):
+        at = pl.ds(pl.multiple_of(i * step_rows, step_rows), step_rows)
+        scaled = acc[at, :] * gain_row
+        inv = inverse[at, 0:1]
+        unit = saved_v[at, :].astype(F32) * inv
+        centre = jnp.mean(scaled * unit, axis=-1, keepdims=True)
+        cot_v[at, :] = (cot_v[at, :].astype(F32) + inv * (scaled - unit * centre)).astype(BF16)
+        return carry
+
+    lax.fori_loop(0, tokens // step_rows, grad_body, 0)
+    send("backward", cot_v, rows_b, (xm, p))
+
     def add(target, lo, count, extra):
         size = 16
 
@@ -312,18 +329,6 @@
         add(terms.at[2, z], H, H, half_a.at[1, z])
     send("tA-", terms.at[2, :, pl.ds(0, A)], side_a.at[1], left)
 
-    def grad_body(i, carry):
-        at = pl.ds(pl.multiple_of(i * step_rows, step_rows), step_rows)
-        scaled = acc[at, :] * gain_row
-        inv = inverse[at, 0:1]
-        unit = saved_v[at, :].astype(F32) * inv
-        centre = jnp.mean(scaled * unit, axis=-1, keepdims=True)
-        cot_v[at, :] = (cot_v[at, :].astype(F32) + inv * (scaled - unit * centre)).astype(BF16)
-        return carry
-
-    lax.fori_loop(0, tokens // step_rows, grad_body, 0)
-    send("backward", cot_v, rows_b, (sm, p))
-
     for k, tag, lo, count, device in ((1, "tb0", A, M - A, right), (2, "tb1", M, shard - M, left)):
         arrive("tB%d" % k, far_b.at[k])
         add(terms.at[k, zh], A, shard - A, far_b.at[k])
@@ -337,7 +342,7 @@
         def build(i, carry):
             at = pl.ds(pl.multiple_of(i * size, size), size)
             row = lax.broadcasted_iota(jnp.int32, (size, tokens), 0) + i * size
-            perm[at, :] = jnp.where(row == where[0:1, :], 1.0, 0.0).astype(BF16)
+            perm[at, :] = jnp.where(row == where, 1.0, 0.0).astype(BF16)
             return carry
 
         lax.fori_loop(0, perm.shape[0] // size, build, 0)
@@ -356,21 +361,42 @@
     def place(ref, number, offset=0):
         return ref.at[pl.ds(pl.multiple_of(offset + number * share, 16), share)]
 
-    def scatter(name, out, offset, sem):
-        local = pltpu.make_async_copy(place(full, p, offset), place(out, p), local_sem.at[sem])
+    def scatter(name, out, offset, sem, flip):
+        section = jnp.where(flip, flipped, s)
         for i, (dz, dy, dc) in enumerate(ORDER):
-            to = peer(zh ^ dz, lax.rem(y + dy, 4), c ^ dc)
-            send("%s%d" % (name, i), place(full, to[1], offset), place(out, p), to)
-        local.start()
-        return local
-
-    def collect(name, out):
+            to = peer(zh ^ dz, lax.rem(y + dy, 4), c ^ dc)[1]
+            send("%s%d" % (name, i), place(full, to, offset), place(out, p), (section, to))
+        away = pltpu.make_async_remote_copy(
+            src_ref=place(full, p, offset), dst_ref=place(out, p), send_sem=send_sem.at[slot(name)],
+            recv_sem=recv_sem.at[slot(name)], device_id=(flipped, p), device_id_type=MESH,
+        )
+        stay = pltpu.make_async_copy(place(full, p, offset), place(out, p), local_sem.at[sem])
+
+        @pl.when(flip)
+        def _():
+            away.start()
+
+        @pl.when(jnp.logical_not(flip))
+        def _():
+            stay.start()
+
+        return away, stay, flip
+
+    def collect(name, out, own):
         for i, (dz, dy, dc) in enumerate(ORDER):
-            origin = peer(zh ^ dz, lax.rem(y + 4 - dy, 4), c ^ dc)
-            arrive("%s%d" % (name, i), place(out, origin[1]))
-
-    for copy in gathered:
-        copy.wait_send()
+            origin = peer(zh ^ dz, lax.rem(y + 4 - dy, 4), c ^ dc)[1]
+            arrive("%s%d" % (name, i), place(out, origin))
+        away, stay, flip = own
+
+        @pl.when(flip)
+        def _():
+            away.wait()
+
+        @pl.when(jnp.logical_not(flip))
+        def _():
+            stay.wait()
+
+    finished(*gathered)
 
     arrive("tA+", side_a.at[0])
     arrive("tA-", side_a.at[1])
@@ -379,13 +405,16 @@
         add(terms.at[3, z], 0, A, side_a.at[1, z])
     send("tzA", terms.at[3, zo, pl.ds(0, A)], far_a, across)
 
+    arrive("flip", targets_flip)
     arrive("forward", rows_f)
-    pack(rows_f, targets, 0)
-    local_f = scatter("f", next_acts, 0, 4)
+    pack(rows_f, jnp.where(x == 0, targets_flip[0:1, :], targets[0:1, :]), 0)
+    finished("backward")
+    own_f = scatter("f", next_acts, 0, 4, x == 0)
     arrive("targets", targets_next)
     arrive("backward", rows_b)
-    pack(rows_b, targets_next, perm.shape[0])
-    local_b = scatter("b", next_grads, perm.shape[0], 5)
+    pack(rows_b, targets_next[0:1, :], perm.shape[0])
+    finished(*["f%d" % i for i in range(len(ORDER))])
+    own_b = scatter("b", next_grads, perm.shape[0], 5, x == 3)
 
     arrive("tzA", far_a)
     arrive("tB3", far_b.at[3])
@@ -415,13 +444,10 @@
     store = pltpu.make_async_copy(acc.at[pl.ds(tokens, shard)], wgrad, local_sem.at[6])
     store.start()
 
-    collect("f", next_acts)
-    collect("b", next_grads)
+    collect("f", next_acts, own_f)
+    collect("b", next_grads, own_b)
     store.wait()
-    local_f.wait()
-    local_b.wait()
-    for copy in sent:
-        copy.wait_send()
+    finished(*list(sent))
     assert len(tags) <= SLOTS, len(tags)
 
 
@@ -458,7 +484,7 @@
             v((2, shard - A, width), BF16),
             v((tokens, width), BF16), v((tokens, width), BF16),
             v((packed, tokens), BF16),
-            v((8, tokens), jnp.int32), v((8, tokens), jnp.int32),
+            v((8, tokens), jnp.int32), v((8, tokens), jnp.int32), v((8, tokens), jnp.int32),
             pltpu.SemaphoreType.DMA((SLOTS,)),
             pltpu.SemaphoreType.DMA((SLOTS,)),
             pltpu.SemaphoreType.DMA((8,)),

time: 262 us -> 232 us (0.89)
  Pallas kernels: 252 us -> 221 us
    pallas_call x1, Pallas kernels: 252 us -> 221 us  [local(): pl.pallas_call(kernel, out_shape=(jax.ShapeDtypeStruct((packed, width), B...]
where the time goes in v2:
time: 232 us; the launch traced here: 230 us
  Pallas kernels  221 us (95%)
  local copies, waits for them, and re-layouts  8.22 us (4%)
    pallas_call x1, Pallas kernels, local(): pl.pallas_call(kernel, out_shape=(jax.ShapeDtypeStruct((packed, width), B...  221 us
    unnamed x7, local copies, waits for them, and re-layouts  8.22 us

profile of v2, /device:TPU:6, one launch (start us, length us, event | category | flops | bytes accessed | tf_op | source)
XLA Modules:
  0.0 229.5 jit_solution(12605687249104333603)
XLA Ops:
  0.6 220.7 %tick.1 = (bf16[768,2560]{1,0:T(8,128)(2,1)}, bf16[768,2560]{1,0:T(8,128)(2,1)}, f32[160,2560]{1,0:T(8,128)}) custom-call(bf16[384,2560]{1,0:T(8,128)(2,1)} %bitcast.10, bf16[384,2560]{1,0:T(8,128)(2,1)} %bitcast.11, bf16[384,2560]{1,0:T(8,128)(2,1)} %bitcast.12, bf16[160,2560]{1,0:T(8,128)(2,1)} %bitcast.14, f32[1,2560]{1,0:T(1,128)} %gain.1, s32[16]{0:T(128)} %bitcast.15), custom_call_target="tpu_custom_call" | custom-call | tf_op jit(solution)/shard_map/tick/pallas_call | solution.py:461
  221.3 0.0 copy-start
  221.3 4.4 %copy.12 = bf16[1,1,768,2560]{3,2,1,0:T(8,128)(2,1)} copy(bf16[1,1,768,2560]{3,2,1,0:T(8,128)(2,1)} %bitcast.9) | data formatting | bytes 7864320
  225.8 0.0 copy-done
  225.8 0.0 copy-start.1
  225.8 1.9 copy.13
  227.7 0.7 copy-done.1
  228.4 1.2 copy.14
Async XLA Ops:
  221.3 4.5 %copy-start = (bf16[768,2560]{1,0:T(8,128)(2,1)S(1)}, bf16[768,2560]{1,0:T(8,128)(2,1)}, u32[]{:S(2)}) copy-start(bf16[768,2560]{1,0:T(8,128)(2,1)} %get-tuple-element.7) | copy-start | bytes 11796484
  225.8 2.6 %copy-start.1 = (f32[160,2560]{1,0:T(8,128)S(1)}, f32[160,2560]{1,0:T(8,128)}, u32[]{:S(2)}) copy-start(f32[160,2560]{1,0:T(8,128)} %get-tuple-element.8) | copy-start | bytes 4915204

commit v3 on v2

--- a/solution.py
+++ b/solution.py
@@ -20,6 +20,7 @@
     (0, 3, 0), (1, 3, 1), (0, 1, 0), (0, 2, 1), (1, 0, 0), (1, 0, 1), (0, 0, 1),
 )
 SLOTS = 96
+STEPS = 4
 
 
 def kernel(
@@ -167,14 +168,14 @@
 
     columns = 512
 
-    def multiply(zz, yy, start=False):
+    def multiply(zz, yy, start=False, part_rows=slice(None)):
         k = zz * 4 + yy
         at = pl.ds(pl.multiple_of(k * chip, 64), chip)
 
         def body(i, carry):
             cols = pl.ds(pl.multiple_of(i * columns, columns), columns)
-            part = jnp.dot(chunks[k], full[at, cols], preferred_element_type=F32)
-            acc[:, cols] = part if start else acc[:, cols] + part
+            part = jnp.dot(chunks[k, part_rows, :], full[at, cols], preferred_element_type=F32)
+            acc[part_rows, cols] = part if start else acc[part_rows, cols] + part
             return carry
 
         lax.fori_loop(0, width // columns, body, 0)
@@ -226,7 +227,7 @@
     pass_on("wA0")
     pass_on("wA1")
     from_core("wA0", "wA1", "zB0", "zB1")
-    multiply(zo, y2)
+    multiply(zo, y2, part_rows=slice(0, tokens))
 
     loads[2].wait()
     gathered = list(sent)
@@ -240,6 +241,8 @@
 
     lax.fori_loop(0, tokens // step_rows, slope_body, 0)
     send("slope", slopes.at[pl.ds(0, tokens)], slopes.at[pl.ds(tokens, tokens)], core)
+
+    multiply(zo, y2, part_rows=slice(tokens, None))
 
     def output_body(i, carry):
         at = pl.ds(pl.multiple_of(i * step_rows, step_rows), step_rows)
@@ -449,6 +452,12 @@
     store.wait()
     finished(*list(sent))
     assert len(tags) <= SLOTS, len(tags)
+
+
+def move(acts, grads, sums, next_acts, next_grads, wgrad):
+    next_acts[...] = acts[...]
+    next_grads[...] = grads[...]
+    wgrad[...] = sums[...]
 
 
 def local(acts, saved, cotangent, weight, gain, route):
@@ -494,6 +503,17 @@
         ),
         name="tick",
     )(acts[0, 0], saved[0, 0], cotangent[0, 0], weight[0], gain, route[0, 0, :, 0])
+    moved = (next_acts, next_grads, weight_grad)
+    specs = [pl.BlockSpec((v.shape[0] // STEPS, width), lambda i: (i, 0)) for v in moved]
+    next_acts, next_grads, weight_grad = pl.pallas_call(
+        move,
+        out_shape=tuple(jax.ShapeDtypeStruct(v.shape, v.dtype) for v in moved),
+        grid=(STEPS,),
+        in_specs=specs,
+        out_specs=tuple(specs),
+        compiler_params=pltpu.CompilerParams(vmem_limit_bytes=62 << 20),
+        name="move",
+    )(*moved)
     return (next_acts[None, None], next_grads[None, None], weight_grad[None])
 
 

time: 232 us -> 230 us (level)
  local copies, waits for them, and re-layouts: 8.22 us -> 0 us
  Pallas kernels: 221 us -> 227 us
    unnamed x7 -> x0, local copies, waits for them, and re-layouts: 8.22 us -> none
    pallas_call x0 -> x1, Pallas kernels: none -> 7.55 us  [local(): pl.pallas_call(move, out_shape=tuple((jax.ShapeDtypeStruct(v.shape, v.dty...]
where the time goes in v3:
time: 230 us; the launch traced here: 228 us
  Pallas kernels  227 us (99%)
    pallas_call x1, Pallas kernels, local(): pl.pallas_call(kernel, out_shape=(jax.ShapeDtypeStruct((packed, width), B...  220 us
    pallas_call x1, Pallas kernels, local(): pl.pallas_call(move, out_shape=tuple((jax.ShapeDtypeStruct(v.shape, v.dty...  7.55 us

profile of v3, /device:TPU:6, one launch (start us, length us, event | category | flops | bytes accessed | tf_op | source)
XLA Modules:
  0.0 228.0 jit_solution(16752888003835356455)
XLA Ops:
  0.6 219.8 %tick.1 = (bf16[768,2560]{1,0:T(8,128)(2,1)}, bf16[768,2560]{1,0:T(8,128)(2,1)}, f32[160,2560]{1,0:T(8,128)}) custom-call(bf16[384,2560]{1,0:T(8,128)(2,1)} %bitcast.8, bf16[384,2560]{1,0:T(8,128)(2,1)} %bitcast.9, bf16[384,2560]{1,0:T(8,128)(2,1)} %bitcast.10, bf16[160,2560]{1,0:T(8,128)(2,1)} %bitcast.11, f32[1,2560]{1,0:T(1,128)} %gain.1, s32[16]{0:T(128)} %bitcast.12), custom_call_target="tpu_custom_call" | custom-call | tf_op jit(solution)/shard_map/tick/pallas_call | solution.py:470
  220.4 7.6 %move.1 = (bf16[768,2560]{1,0:T(8,128)(2,1)}, bf16[768,2560]{1,0:T(8,128)(2,1)}, f32[160,2560]{1,0:T(8,128)}) custom-call(bf16[768,2560]{1,0:T(8,128)(2,1)} %get-tuple-element.9.acts, bf16[768,2560]{1,0:T(8,128)(2,1)} %get-tuple-element.10.grads, f32[160,2560]{1,0:T(8,128)} %get-tuple-element.11.sums), custom_call_target="tpu_custom_call" | custom-call | tf_op jit(solution)/shard_map/move/pallas_call | solution.py:508

commit v4 on v3

--- a/solution.py
+++ b/solution.py
@@ -239,8 +239,10 @@
         slopes[at, :] = (cot_v[at, :].astype(F32) * (sigma * (1.0 + v * (1.0 - sigma)))).astype(BF16)
         return carry
 
-    lax.fori_loop(0, tokens // step_rows, slope_body, 0)
-    send("slope", slopes.at[pl.ds(0, tokens)], slopes.at[pl.ds(tokens, tokens)], core)
+    third = tokens // 3
+    for i in range(3):
+        lax.fori_loop(i * third // step_rows, (i + 1) * third // step_rows, slope_body, 0)
+        send("slope%d" % i, slopes.at[pl.ds(i * third, third)], slopes.at[pl.ds(tokens + i * third, third)], core)
 
     multiply(zo, y2, part_rows=slice(tokens, None))
 
@@ -254,7 +256,8 @@
     send("forward", acts_v, rows_f, (xp, p))
 
     arrive("turned", turned.at[:, pl.ds(tokens, tokens)])
-    arrive("slope", slopes.at[pl.ds(tokens, tokens)])
+    for i in range(3):
+        arrive("slope%d" % i, slopes.at[pl.ds(tokens + i * third, third)])
 
     def term(k, yy):
         at = pl.ds(pl.multiple_of(yy * chip, 64), chip)

time: 230 us -> 229 us (level)
  no operation moved by 1% of the time
where the time goes in v4:
time: 229 us; the launch traced here: 227 us
  Pallas kernels  226 us (99%)
    pallas_call x1, Pallas kernels, local(): pl.pallas_call(kernel, out_shape=(jax.ShapeDtypeStruct((packed, width), B...  219 us
    pallas_call x1, Pallas kernels, local(): pl.pallas_call(move, out_shape=tuple((jax.ShapeDtypeStruct(v.shape, v.dty...  7.55 us

profile of v4, /device:TPU:6, one launch (start us, length us, event | category | flops | bytes accessed | tf_op | source)
XLA Modules:
  0.0 227.0 jit_solution(10932953098573021779)
XLA Ops:
  0.6 218.8 %tick.1 = (bf16[768,2560]{1,0:T(8,128)(2,1)}, bf16[768,2560]{1,0:T(8,128)(2,1)}, f32[160,2560]{1,0:T(8,128)}) custom-call(bf16[384,2560]{1,0:T(8,128)(2,1)} %bitcast.8, bf16[384,2560]{1,0:T(8,128)(2,1)} %bitcast.9, bf16[384,2560]{1,0:T(8,128)(2,1)} %bitcast.10, bf16[160,2560]{1,0:T(8,128)(2,1)} %bitcast.11, f32[1,2560]{1,0:T(1,128)} %gain.1, s32[16]{0:T(128)} %bitcast.12), custom_call_target="tpu_custom_call" | custom-call | tf_op jit(solution)/shard_map/tick/pallas_call | solution.py:473
  219.4 7.6 %move.1 = (bf16[768,2560]{1,0:T(8,128)(2,1)}, bf16[768,2560]{1,0:T(8,128)(2,1)}, f32[160,2560]{1,0:T(8,128)}) custom-call(bf16[768,2560]{1,0:T(8,128)(2,1)} %get-tuple-element.9.acts, bf16[768,2560]{1,0:T(8,128)(2,1)} %get-tuple-element.10.grads, f32[160,2560]{1,0:T(8,128)} %get-tuple-element.11.sums), custom_call_target="tpu_custom_call" | custom-call | tf_op jit(solution)/shard_map/move/pallas_call | solution.py:511

commit v5 on v4

--- a/solution.py
+++ b/solution.py
@@ -19,7 +19,7 @@
     (1, 2, 0), (1, 2, 1), (0, 2, 0), (1, 1, 0), (0, 3, 1), (1, 3, 0), (0, 1, 1), (1, 1, 1),
     (0, 3, 0), (1, 3, 1), (0, 1, 0), (0, 2, 1), (1, 0, 0), (1, 0, 1), (0, 0, 1),
 )
-SLOTS = 96
+SLOTS = 104
 STEPS = 4
 
 
@@ -252,8 +252,10 @@
         acts_v[at, :] = (acts_v[at, :].astype(F32) + v * jax.nn.sigmoid(v)).astype(BF16)
         return carry
 
-    lax.fori_loop(0, tokens // step_rows, output_body, 0)
-    send("forward", acts_v, rows_f, (xp, p))
+    for i in range(3):
+        part = pl.ds(i * third, third)
+        lax.fori_loop(i * third // step_rows, (i + 1) * third // step_rows, output_body, 0)
+        send("forward%d" % i, acts_v.at[part], rows_f.at[part], (xp, p))
 
     arrive("turned", turned.at[:, pl.ds(tokens, tokens)])
     for i in range(3):
@@ -308,8 +310,10 @@
         cot_v[at, :] = (cot_v[at, :].astype(F32) + inv * (scaled - unit * centre)).astype(BF16)
         return carry
 
-    lax.fori_loop(0, tokens // step_rows, grad_body, 0)
-    send("backward", cot_v, rows_b, (xm, p))
+    for i in range(3):
+        part = pl.ds(i * third, third)
+        lax.fori_loop(i * third // step_rows, (i + 1) * third // step_rows, grad_body, 0)
+        send("backward%d" % i, cot_v.at[part], rows_b.at[part], (xm, p))
 
     def add(target, lo, count, extra):
         size = 16
@@ -412,12 +416,14 @@
     send("tzA", terms.at[3, zo, pl.ds(0, A)], far_a, across)
 
     arrive("flip", targets_flip)
-    arrive("forward", rows_f)
+    for i in range(3):
+        arrive("forward%d" % i, rows_f.at[pl.ds(i * third, third)])
     pack(rows_f, jnp.where(x == 0, targets_flip[0:1, :], targets[0:1, :]), 0)
-    finished("backward")
+    finished("backward0", "backward1", "backward2")
     own_f = scatter("f", next_acts, 0, 4, x == 0)
     arrive("targets", targets_next)
-    arrive("backward", rows_b)
+    for i in range(3):
+        arrive("backward%d" % i, rows_b.at[pl.ds(i * third, third)])
     pack(rows_b, targets_next[0:1, :], perm.shape[0])
     finished(*["f%d" % i for i in range(len(ORDER))])
     own_b = scatter("b", next_grads, perm.shape[0], 5, x == 3)

time: 229 us -> 227 us (level)
  no operation moved by 1% of the time
where the time goes in v5:
time: 227 us; the launch traced here: 225 us
  Pallas kernels  225 us (99%)
    pallas_call x1, Pallas kernels, local(): pl.pallas_call(kernel, out_shape=(jax.ShapeDtypeStruct((packed, width), B...  217 us
    pallas_call x1, Pallas kernels, local(): pl.pallas_call(move, out_shape=tuple((jax.ShapeDtypeStruct(v.shape, v.dty...  7.55 us

profile of v5, /device:TPU:6, one launch (start us, length us, event | category | flops | bytes accessed | tf_op | source)
XLA Modules:
  0.0 225.3 jit_solution(966168443896715736)
XLA Ops:
  0.6 217.1 %tick.1 = (bf16[768,2560]{1,0:T(8,128)(2,1)}, bf16[768,2560]{1,0:T(8,128)(2,1)}, f32[160,2560]{1,0:T(8,128)}) custom-call(bf16[384,2560]{1,0:T(8,128)(2,1)} %bitcast.8, bf16[384,2560]{1,0:T(8,128)(2,1)} %bitcast.9, bf16[384,2560]{1,0:T(8,128)(2,1)} %bitcast.10, bf16[160,2560]{1,0:T(8,128)(2,1)} %bitcast.11, f32[1,2560]{1,0:T(1,128)} %gain.1, s32[16]{0:T(128)} %bitcast.12), custom_call_target="tpu_custom_call" | custom-call | tf_op jit(solution)/shard_map/tick/pallas_call | solution.py:479
  217.8 7.6 %move.1 = (bf16[768,2560]{1,0:T(8,128)(2,1)}, bf16[768,2560]{1,0:T(8,128)(2,1)}, f32[160,2560]{1,0:T(8,128)}) custom-call(bf16[768,2560]{1,0:T(8,128)(2,1)} %get-tuple-element.9.acts, bf16[768,2560]{1,0:T(8,128)(2,1)} %get-tuple-element.10.grads, f32[160,2560]{1,0:T(8,128)} %get-tuple-element.11.sums), custom_call_target="tpu_custom_call" | custom-call | tf_op jit(solution)/shard_map/move/pallas_call | solution.py:517

commit v6 on v3

--- a/solution.py
+++ b/solution.py
@@ -19,7 +19,7 @@
     (1, 2, 0), (1, 2, 1), (0, 2, 0), (1, 1, 0), (0, 3, 1), (1, 3, 0), (0, 1, 1), (1, 1, 1),
     (0, 3, 0), (1, 3, 1), (0, 1, 0), (0, 2, 1), (1, 0, 0), (1, 0, 1), (0, 0, 1),
 )
-SLOTS = 96
+SLOTS = 120
 STEPS = 4
 
 
@@ -239,8 +239,10 @@
         slopes[at, :] = (cot_v[at, :].astype(F32) * (sigma * (1.0 + v * (1.0 - sigma)))).astype(BF16)
         return carry
 
-    lax.fori_loop(0, tokens // step_rows, slope_body, 0)
-    send("slope", slopes.at[pl.ds(0, tokens)], slopes.at[pl.ds(tokens, tokens)], core)
+    sixth = tokens // 6
+    for i in range(6):
+        lax.fori_loop(i * sixth // step_rows, (i + 1) * sixth // step_rows, slope_body, 0)
+        send("slope%d" % i, slopes.at[pl.ds(i * sixth, sixth)], slopes.at[pl.ds(tokens + i * sixth, sixth)], core)
 
     multiply(zo, y2, part_rows=slice(tokens, None))
 
@@ -250,11 +252,14 @@
         acts_v[at, :] = (acts_v[at, :].astype(F32) + v * jax.nn.sigmoid(v)).astype(BF16)
         return carry
 
-    lax.fori_loop(0, tokens // step_rows, output_body, 0)
-    send("forward", acts_v, rows_f, (xp, p))
+    for i in range(6):
+        part = pl.ds(i * sixth, sixth)
+        lax.fori_loop(i * sixth // step_rows, (i + 1) * sixth // step_rows, output_body, 0)
+        send("forward%d" % i, acts_v.at[part], rows_f.at[part], (xp, p))
 
     arrive("turned", turned.at[:, pl.ds(tokens, tokens)])
-    arrive("slope", slopes.at[pl.ds(tokens, tokens)])
+    for i in range(6):
+        arrive("slope%d" % i, slopes.at[pl.ds(tokens + i * sixth, sixth)])
 
     def term(k, yy):
         at = pl.ds(pl.multiple_of(yy * chip, 64), chip)
@@ -305,8 +310,10 @@
         cot_v[at, :] = (cot_v[at, :].astype(F32) + inv * (scaled - unit * centre)).astype(BF16)
         return carry
 
-    lax.fori_loop(0, tokens // step_rows, grad_body, 0)
-    send("backward", cot_v, rows_b, (xm, p))
+    for i in range(6):
+        part = pl.ds(i * sixth, sixth)
+        lax.fori_loop(i * sixth // step_rows, (i + 1) * sixth // step_rows, grad_body, 0)
+        send("backward%d" % i, cot_v.at[part], rows_b.at[part], (xm, p))
 
     def add(target, lo, count, extra):
         size = 16
@@ -409,12 +416,14 @@
     send("tzA", terms.at[3, zo, pl.ds(0, A)], far_a, across)
 
     arrive("flip", targets_flip)
-    arrive("forward", rows_f)
+    for i in range(6):
+        arrive("forward%d" % i, rows_f.at[pl.ds(i * sixth, sixth)])
     pack(rows_f, jnp.where(x == 0, targets_flip[0:1, :], targets[0:1, :]), 0)
-    finished("backward")
+    finished(*["backward%d" % i for i in range(6)])
     own_f = scatter("f", next_acts, 0, 4, x == 0)
     arrive("targets", targets_next)
-    arrive("backward", rows_b)
+    for i in range(6):
+        arrive("backward%d" % i, rows_b.at[pl.ds(i * sixth, sixth)])
     pack(rows_b, targets_next[0:1, :], perm.shape[0])
     finished(*["f%d" % i for i in range(len(ORDER))])
     own_b = scatter("b", next_grads, perm.shape[0], 5, x == 3)

time: 230 us -> 227 us (0.987)
  Pallas kernels: 227 us -> 224 us
    pallas_call x1, Pallas kernels: 220 us -> 217 us  [local(): pl.pallas_call(kernel, out_shape=(jax.ShapeDtypeStruct((packed, width), B...]
where the time goes in v6:
time: 227 us; the launch traced here: 225 us
  Pallas kernels  224 us (99%)
    pallas_call x1, Pallas kernels, local(): pl.pallas_call(kernel, out_shape=(jax.ShapeDtypeStruct((packed, width), B...  217 us
    pallas_call x1, Pallas kernels, local(): pl.pallas_call(move, out_shape=tuple((jax.ShapeDtypeStruct(v.shape, v.dty...  7.55 us

profile of v6, /device:TPU:6, one launch (start us, length us, event | category | flops | bytes accessed | tf_op | source)
XLA Modules:
  0.0 224.8 jit_solution(11858657081213220688)
XLA Ops:
  0.6 216.6 %tick.1 = (bf16[768,2560]{1,0:T(8,128)(2,1)}, bf16[768,2560]{1,0:T(8,128)(2,1)}, f32[160,2560]{1,0:T(8,128)}) custom-call(bf16[384,2560]{1,0:T(8,128)(2,1)} %bitcast.8, bf16[384,2560]{1,0:T(8,128)(2,1)} %bitcast.9, bf16[384,2560]{1,0:T(8,128)(2,1)} %bitcast.10, bf16[160,2560]{1,0:T(8,128)(2,1)} %bitcast.11, f32[1,2560]{1,0:T(1,128)} %gain.1, s32[16]{0:T(128)} %bitcast.12), custom_call_target="tpu_custom_call" | custom-call | tf_op jit(solution)/shard_map/tick/pallas_call | solution.py:479
  217.3 7.6 %move.1 = (bf16[768,2560]{1,0:T(8,128)(2,1)}, bf16[768,2560]{1,0:T(8,128)(2,1)}, f32[160,2560]{1,0:T(8,128)}) custom-call(bf16[768,2560]{1,0:T(8,128)(2,1)} %get-tuple-element.9.acts, bf16[768,2560]{1,0:T(8,128)(2,1)} %get-tuple-element.10.grads, f32[160,2560]{1,0:T(8,128)} %get-tuple-element.11.sums), custom_call_target="tpu_custom_call" | custom-call | tf_op jit(solution)/shard_map/move/pallas_call | solution.py:517
